TPU v7x, 32 devices: a whole 2x2x4 slice. The times are simulated.
32 devices in a mesh: rep: 2 (over x), seq: 16 (over z, y, core).
Axes of the slice: x: 2, y: 2, z: 4, core: 2. Of those that a mesh axis runs over, the one named last changes fastest.
Arguments:
- tokens: bfloat16 [256, 12288], P('rep', 'seq'), parts along dimension 0, may hold values from -6 to 6
- w_query: bfloat16 [12288, 12288], P(None, 'seq'), may hold values from -0.0546875 to 0.0546875
- w_key_value: bfloat16 [12288, 2048], P('seq'), may hold values from -0.0546875 to 0.0546875
- w_out: bfloat16 [12288, 12288], P('seq'), may hold values from -0.078125 to 0.078125
- cache_keys: bfloat16 [16384, 1024], P(('rep', 'seq')), parts along dimension 0, as said below
- cache_values: bfloat16 [16384, 1024], P(('rep', 'seq')), parts along dimension 0, may hold values from -6 to 6
- lengths: int32 [32], P(('rep', 'seq')), parts along dimension 0, may hold values from 128 to 512, as said below
- offset: int32 [2], P('rep'), parts along dimension 0, may hold values from 6144 to 8192
Outputs:
- mixed: bfloat16 [256, 12288], P('rep', 'seq'), parts along dimension 0
There are 2 independent parts, one for each index of `rep`. A program takes and returns all parts, laid end to end along the dimension named above; an argument that names none is the same for every part. Nothing has to cross between parts.
Inputs may be any that keep to these rules, and one draw needn't show every extreme that they name: `lengths`: every block of 512 slots has between 128 and 512 filled slots; some block is full. `cache_keys`: entries lie within -100 and 100.
All inputs are finite; a program needn't handle non-finite values.
Results may differ from a plain program's by a relative error of at most 0.0087.
Values may be sent and summed in bfloat16 or wider, within the bound.
A program may use at most 192 MiB of HBM per device.

v0:
```python
import jax
import jax.numpy as jnp
from jax import lax
from jax.sharding import PartitionSpec as P

E = 128


NEGATIVE_FILL = -1e30


def local(tokens, w_query, w_key_value, w_out, cache_keys, cache_values, lengths, offset):
    devices = lax.axis_size("seq")
    own_index = lax.axis_index("seq")
    span_rows = tokens.shape[0]
    kv_columns = cache_keys.shape[1]
    kv_heads = kv_columns // E
    cache_rows = cache_keys.shape[0]
    token_index = jnp.arange(span_rows, dtype=jnp.int32)
    projected = jnp.dot(
        lax.all_gather(tokens, "seq", axis=1, tiled=True),
        w_query,
        preferred_element_type=jnp.float32,
    )
    local_queries = (projected * E ** (-0.5)).astype(jnp.bfloat16)
    queries = lax.all_gather(local_queries, "seq", axis=1, tiled=True)
    heads_all = queries.shape[1] // E
    group_size = heads_all // kv_heads
    summed_rows = lax.psum(jnp.dot(tokens, w_key_value, preferred_element_type=jnp.float32), "seq")
    fresh_rows = summed_rows.astype(jnp.bfloat16)
    fresh_index = jnp.arange(span_rows, dtype=jnp.int32)
    fresh_live = jnp.broadcast_to(own_index == devices - 1, (span_rows,))
    all_keys = jnp.concatenate([cache_keys, fresh_rows[:, :kv_columns]], 0)
    all_values = jnp.concatenate([cache_values, fresh_rows[:, kv_columns:]], 0)
    cache_slot = jnp.arange(cache_rows, dtype=jnp.int32)
    cache_live = (cache_slot < lengths[0]) & (own_index * cache_rows + cache_slot < offset[0])
    fresh_seen = (fresh_index[None, :] <= token_index[:, None]) & fresh_live[None, :]
    visible = jnp.concatenate(
        [jnp.broadcast_to(cache_live[None, :], (span_rows, cache_rows)), fresh_seen], 1
    )
    query_heads = queries.reshape(span_rows, kv_heads, group_size, E)
    key_heads = all_keys.reshape(-1, kv_heads, E)
    value_heads = all_values.reshape(-1, kv_heads, E)
    scores = jnp.einsum(
        "qhge,phe->hgqp", query_heads, key_heads, preferred_element_type=jnp.float32
    )
    scores = jnp.where(visible, scores, NEGATIVE_FILL)
    local_highest = jnp.max(scores, axis=-1)
    highest = lax.pmax(local_highest, "seq")
    exponent = jnp.where(visible, jnp.exp(scores - highest[..., None]), 0.0)
    local_totals = jnp.sum(exponent, axis=-1)
    weights = exponent.astype(jnp.bfloat16)
    numerator = jnp.einsum(
        "hgqp,phe->qhge", weights, value_heads, preferred_element_type=jnp.float32
    ).reshape(span_rows, heads_all * E)
    totals = lax.psum(local_totals, "seq")
    per_column = jnp.repeat(totals.reshape(heads_all, span_rows).T, E, axis=1)
    summed = lax.psum_scatter(numerator, "seq", scatter_dimension=1, tiled=True)
    col_count = summed.shape[1]
    divisor = lax.dynamic_slice_in_dim(per_column, own_index * col_count, col_count, 1)
    attention = (summed / divisor).astype(jnp.bfloat16)
    output_sum = lax.psum_scatter(
        jnp.dot(attention, w_out, preferred_element_type=jnp.float32),
        "seq",
        scatter_dimension=1,
        tiled=True,
    )
    return output_sum.astype(jnp.bfloat16)


def solution(mesh):
    in_specs = (
        P("rep", "seq"),
        P(None, "seq"),
        P("seq", None),
        P("seq", None),
        P(("rep", "seq"), None),
        P(("rep", "seq"), None),
        P(("rep", "seq")),
        P("rep"),
    )
    out_specs = P("rep", "seq")
    return jax.shard_map(local, mesh=mesh, in_specs=in_specs, out_specs=out_specs, check_vma=False)
```

profile of v0, /device:TPU:0, one launch (start us, length us, event | category | flops | bytes accessed | tf_op | source)
XLA Modules:
  0.0 434.4 jit_solution(12853956449923015528)
XLA Ops:
  6.5 0.0 copy-start
  6.5 0.0 all-gather.3.cloned.1.call-start
  6.5 0.7 all-gather.3.cloned.1.call-update
  7.3 0.0 copy-start.2
  7.3 0.0 all-gather.5.cloned.1.call-start
  7.3 50.6 %all-gather.3.cloned.1.call-done = bf16[128,12288]{1,0:T(8,128)(2,1)} async-done(((bf16[128,768]{1,0:T(8,128)(2,1)}), bf16[128,12288]{1,0:T(8,128)(2,1)}) %all-gather.3.cloned.1.call-update) | async-done | bytes 3145744 | tf_op jit(solution)/shard_map/all_gather | solution.py:21
  57.9 10.6 %fusion.6 = bf16[128,768]{1,0:T(8,128)(2,1)} fusion(bf16[128,12288]{1,0:T(8,128)(2,1)} %all-gather.3.cloned.1.call-done, bf16[12288,768]{1,0:T(8,128)(2,1)} %param.9), kind=kOutput, calls=%fused_computation.10 | convolution fusion | flops 2416115712 | bytes 22216704 | tf_op jit(solution)/shard_map/dot_general | solution.py:20
  68.5 0.0 all-gather.5.cloned.1.call-update
  68.5 0.0 reduce-scatter.3.cloned.1.call-start
  69.9 0.0 copy-done
  69.9 0.0 copy-done.2
  69.9 1.6 fusion.14
  71.5 77.5 %all-reduce.1 = bf16[128,2048]{1,0:T(8,128)(2,1)S(1)} all-reduce(f32[128,2048]{1,0:T(8,128)} %fusion.14), channel_id=1, replica_groups=mesh['rep'=2,'seq'=16] {'seq'}, use_global_device_ids=true, to_apply=%region_0.0 | all-reduce | flops 262144 | bytes 1572864 | tf_op jit(solution)/shard_map/psum | solution.py:29
  149.1 0.2 copy.14
  149.2 1.5 copy.13
  150.7 1.3 pad_maximum_fusion
  152.1 1.5 copy.12
  153.6 1.2 pad_maximum_fusion.1
  154.8 0.1 pad_add_fusion
  154.9 0.0 all-gather.5.cloned.1.call-done
  155.0 3.5 copy.15
  158.5 13.7 %fusion = (f32[8,12,128]{2,1,0:T(8,128)S(1)}, f32[8,640,128,12]{2,1,3,0:T(8,128)}) fusion(pred[128,640]{0,1:T(8,128)(4,1)S(1)} %pad_add_fusion, bf16[640,8,128,1]{0,2,3,1:T(8,128)(2,1)} %bitcast.41, bf16[128,8,12,128]{0,3,2,1:T(8,128)(2,1)S(1)} %bitcast.39), kind=kOutput, calls=%fused_computation.2 | convolution fusion | flops 2028982272 | bytes 36044800 | tf_op jit(solution)/shard_map/qhge,phe->hgqp/dot_general | solution.py:44
  172.2 57.7 %pmax.7 = f32[8,12,128]{2,1,0:T(8,128)S(1)} all-reduce(f32[8,12,128]{2,1,0:T(8,128)S(1)} %get-tuple-element.7), channel_id=1, replica_groups=mesh['rep'=2,'seq'=16] {'seq'}, use_global_device_ids=true, to_apply=%region_2.3 | all-reduce | flops 12288 | bytes 98304 | tf_op jit(solution)/shard_map/pmax | solution.py:49
  229.8 15.8 %fusion.3 = f32[8,128,12,128]{3,1,2,0:T(8,128)} fusion(bf16[640,8,128,1]{0,2,3,1:T(8,128)(2,1)} %bitcast.43, f32[8,640,128,12]{2,1,3,0:T(8,128)} %get-tuple-element.8, f32[8,12,128]{2,1,0:T(8,128)S(1)} %pmax.7, pred[128,640]{0,1:T(8,128)(4,1)S(1)} %pad_add_fusion), kind=kOutput, calls=%fused_computation.5 | convolution fusion | flops 2044723200 | bytes 39190528 | tf_op jit(solution)/shard_map/hgqp,phe->qhge/dot_general | solution.py:53
  245.6 0.0 reduce-scatter.3.cloned.1.call-update
  245.7 0.0 reduce-scatter.5.cloned.1.call-start
  245.7 14.8 %fusion.1 = f32[8,12,128]{2,1,0:T(8,128)S(1)} fusion(f32[8,640,128,12]{2,1,3,0:T(8,128)} %get-tuple-element.8, f32[8,12,128]{2,1,0:T(8,128)S(1)} %pmax.7, pred[128,640]{0,1:T(8,128)(4,1)S(1)} %pad_add_fusion), kind=kLoop, calls=%fused_computation.3 | loop fusion | flops 31444992 | bytes 31637504 | tf_op jit(solution)/shard_map/reduce_sum | solution.py:51
  260.6 59.4 %psum.15 = f32[128,96]{0,1:T(8,128)S(1)} all-reduce(f32[128,96]{0,1:T(8,128)S(1)} %bitcast.44), channel_id=1, replica_groups=mesh['rep'=2,'seq'=16] {'seq'}, use_global_device_ids=true, to_apply=%region_5.6 | all-reduce | flops 12288 | bytes 98304 | tf_op jit(solution)/shard_map/psum | solution.py:56
  320.0 8.7 %reduce-scatter.3.cloned.1.call-done = f32[128,768]{0,1:T(8,128)} async-done(((f32[128,12288]{0,1:T(8,128)}), f32[128,768]{0,1:T(8,128)}) %reduce-scatter.3.cloned.1.call-update) | async-done | bytes 393232 | tf_op jit(solution)/shard_map/reduce_scatter | solution.py:58
  328.7 0.0 copy-start.3
  328.7 0.4 broadcast_in_dim.28
  329.1 0.6 copy-done.3
  329.7 0.0 copy-start.1
  329.7 12.0 %fusion.7 = f32[128,12288]{1,0:T(8,128)} fusion(bf16[768,12288]{1,0:T(8,128)(2,1)} %param.11, f32[128,768]{0,1:T(8,128)S(1)} %copy-done.3, f32[128,12288]{0,1:T(8,128)S(1)} %bitcast.40, s32[]{:T(128)S(6)} %select_n.12), kind=kOutput, calls=%fused_computation.13 | convolution fusion | flops 2416115712 | bytes 25952260 | tf_op jit(solution)/shard_map/dot_general | solution.py:63
  341.6 0.0 reduce-scatter.5.cloned.1.call-update
  341.6 84.5 %reduce-scatter.5.cloned.1.call-done = f32[128,768]{1,0:T(8,128)} async-done(((f32[128,12288]{1,0:T(8,128)}), f32[128,768]{1,0:T(8,128)}) %reduce-scatter.5.cloned.1.call-update) | async-done | bytes 393232 | tf_op jit(solution)/shard_map/reduce_scatter | solution.py:62
  426.2 1.7 convert_element_type.19
  427.9 0.0 copy-done.1
  (5 shorter events, 0.1 us)
Async XLA Ops:
  6.5 63.4 %copy-start = (bf16[768,2048]{1,0:T(8,128)(2,1)S(1)}, bf16[768,2048]{1,0:T(8,128)(2,1)}, u32[]{:S(2)}) copy-start(bf16[768,2048]{1,0:T(8,128)(2,1)} %param.10) | copy-start | bytes 9437188
  6.5 51.4 %all-gather.3.cloned.1.call-start = ((), (), s32[]{:S(2)}) async-start(), calls=%async_computation.2 | async-start | bytes 3342336 | tf_op jit(solution)/shard_map/all_gather | solution.py:21
  7.3 62.6 %copy-start.2 = (bf16[128,768]{1,0:T(8,128)(2,1)S(1)}, bf16[128,768]{1,0:T(8,128)(2,1)}, u32[]{:S(2)}) copy-start(bf16[128,768]{1,0:T(8,128)(2,1)} %param.8) | copy-start | bytes 589828
  7.3 147.7 %all-gather.5.cloned.1.call-start = ((), (), s32[]{:S(2)}) async-start(), calls=%async_computation.3 | async-start | bytes 3342336 | tf_op jit(solution)/shard_map/all_gather | solution.py:26
  68.5 260.1 %reduce-scatter.3.cloned.1.call-start = ((), (), s32[]{:S(2)}) async-start(), calls=%async_computation.4 | async-start | bytes 6684672 | tf_op jit(solution)/shard_map/reduce_scatter | solution.py:58
  245.7 180.5 %reduce-scatter.5.cloned.1.call-start = ((), (), s32[]{:S(2)}) async-start(), calls=%async_computation.5 | async-start | bytes 6684672 | tf_op jit(solution)/shard_map/reduce_scatter | solution.py:62
  328.7 1.0 copy-start.3
  329.7 98.2 %copy-start.1 = (bf16[768,2048]{1,0:T(8,128)(2,1)S(1)}, bf16[768,2048]{1,0:T(8,128)(2,1)}, u32[]{:S(2)}) copy-start(bf16[768,2048]{1,0:T(8,128)(2,1)} %param.10) | copy-start | bytes 9437188
Sparse Core Ops, SparseCore 0:
  9.6 48.3 all-gather.2
  68.7 49.1 all-gather.4
  245.8 82.8 reduce-scatter.2
  341.8 84.3 reduce-scatter.4
where the time goes:
time: 435 us; the launch traced here: 434 us
  blocking collectives  195 us (45%)
  waiting for transfers between devices  145 us (33%)
  matrix products  53.7 us (12%)
  other arithmetic  19.2 us (4%)
  between operations  14.5 us (3%)
  local copies, waits for them, and re-layouts  7.69 us (2%)
    reduce_scatter x1, waiting for transfers between devices, local(): lax.psum_scatter(jnp.dot(attention, w_out, preferred_element_type=jnp.flo...  84.5 us
    psum x1, blocking collectives, local(): lax.psum(jnp.dot(tokens, w_key_value, preferred_element_type=jnp.float32)...  77.5 us
    psum x1, blocking collectives, local(): totals = lax.psum(local_totals, 'seq')  59.4 us
    pmax x1, blocking collectives, local(): highest = lax.pmax(local_highest, 'seq')  57.7 us
    all_gather x1, waiting for transfers between devices, local(): lax.all_gather(tokens, 'seq', axis=1, tiled=True)  50.6 us
    dot_general x1, matrix products, local(): jnp.einsum('hgqp,phe->qhge', weights, value_heads, preferred_element_type...  15.8 us
    reduce_sum x1, other arithmetic, local(): local_totals = jnp.sum(exponent, axis=-1)  14.8 us
    dot_general x1, matrix products, local(): jnp.einsum('qhge,phe->hgqp', query_heads, key_heads, preferred_element_ty...  13.7 us
  transfers between devices with their start and end apart: 4, of which 3 were waited for; matrix products, arithmetic and copies ran while one was open for 5% of the time, Pallas kernels for 0%

commit v1 on v0

--- a/solution.py
+++ b/solution.py
@@ -1,12 +1,398 @@
 import jax
 import jax.numpy as jnp
 from jax import lax
+from jax.experimental import pallas as pl
+from jax.experimental.pallas import tpu as pltpu
 from jax.sharding import PartitionSpec as P
 
 E = 128
+MASK_ROWS = 16
 
 
 NEGATIVE_FILL = -1e30
+
+
+def kernel(tokens, w_query, w_key_value, w_out, cache_keys, cache_values, lengths, offset, out,
+           tok, weights, w_kv, stage, kv, mine, theirs, fresh_out, fresh_in, fresh, projected, query,
+           high, total, attended, attention, first_out, first_in, second_out, second_in, third_out, third_in,
+           load_sem, weight_sem, tok_send, tok_recv, kv_send, kv_recv, kv_pass, pair_send, pair_recv,
+           fresh_send, fresh_recv, share_send, share_recv, one_send, one_recv, two_send, two_recv,
+           three_send, three_recv):
+    rows, width = tokens.shape
+    slots = cache_keys.shape[0]
+    n_z = tok.shape[0] // 4
+    chips = 2 * n_z
+    half = w_kv.shape[1] // 2
+    group = width // E
+    f32, bf16 = jnp.float32, jnp.bfloat16
+    me = lax.axis_index("seq")
+    core = lax.rem(me, 2)
+    chip = me // 2
+    y = lax.rem(chip, 2)
+    z = chip // 2
+    other = me + 1 - 2 * core
+
+    def index(zz, yy, cc):
+        return (zz * 2 + yy) * 2 + cc
+
+    def shifted(kz):
+        return lax.rem(z + kz, n_z)
+
+    y_peer = index(z, 1 - y, core)
+
+    def remote(src, dst, send, recv, peer):
+        return pltpu.make_async_remote_copy(
+            src_ref=src, dst_ref=dst, send_sem=send, recv_sem=recv,
+            device_id={"seq": peer}, device_id_type=pl.DeviceIdType.MESH)
+
+    own_tokens = pltpu.make_async_copy(tokens, tok.at[me], load_sem.at[0])
+    own_tokens.start()
+    load_kv = pltpu.make_async_copy(w_key_value, w_kv, load_sem.at[1])
+    load_kv.start()
+
+    def query_weight(i):
+        return pltpu.make_async_copy(
+            w_query.at[pl.ds(pl.multiple_of(i * width, width), width), :], weights.at[i], weight_sem.at[i])
+
+    def out_weight(i):
+        return pltpu.make_async_copy(
+            w_out.at[:, pl.ds(pl.multiple_of(i * width, width), width)], weights.at[i], weight_sem.at[i])
+
+    stage_loads = []
+    for head in range(chips):
+        columns = pl.ds(head * E, E)
+        for part, cache in enumerate((cache_keys, cache_values)):
+            stage_loads.append(pltpu.make_async_copy(
+                cache.at[:, columns], stage.at[head, pl.ds(part * slots, slots), :],
+                load_sem.at[2 + 2 * head + part]))
+    own_columns = pl.ds(pl.multiple_of(chip * E, E), E)
+    own_loads = [
+        pltpu.make_async_copy(cache.at[:, own_columns], kv.at[me, pl.ds(part * slots, slots), :],
+                              load_sem.at[2 + 2 * chips + part])
+        for part, cache in enumerate((cache_keys, cache_values))]
+    for load in stage_loads + own_loads:
+        load.start()
+
+    @pl.loop(0, tok.shape[0])
+    def _(i):
+        query_weight(i).start()
+
+    barrier = pltpu.get_barrier_semaphore()
+    peers = [index(shifted(kz), yy, core) for kz in range(n_z) for yy in (y, 1 - y)][1:] + [other]
+    for peer in peers:
+        pl.semaphore_signal(barrier, inc=1, device_id={"seq": peer}, device_id_type=pl.DeviceIdType.MESH)
+    pl.semaphore_wait(barrier, len(peers))
+
+    def tok_copy(i, send, peer):
+        return remote(tok.at[i], tok.at[i], tok_send.at[send], tok_recv.at[i], peer)
+
+    own_tokens.wait()
+    sends = []
+    for kz in range(1, n_z):
+        sends.append(tok_copy(me, kz - 1, index(shifted(kz), y, core)))
+    sends.append(tok_copy(me, n_z - 1, y_peer))
+    sends.append(tok_copy(me, 2 * n_z - 1, other))
+    for copy in sends:
+        copy.start()
+
+    lane = lax.broadcasted_iota(jnp.int32, (MASK_ROWS, E), 0) * E + lax.broadcasted_iota(jnp.int32, (MASK_ROWS, E), 1)
+    seen = (lane < lengths[0]) & (me * slots + lane < offset[0])
+    bias = jnp.where(seen, 0.0, NEGATIVE_FILL).astype(bf16)
+    for head in range(chips):
+        stage[head, pl.ds(2 * slots, MASK_ROWS), :] = bias
+    kv[me, pl.ds(2 * slots, MASK_ROWS), :] = bias
+
+    load_kv.wait()
+    for part in range(2):
+        product = jnp.dot(tok[me], w_kv[:, pl.ds(part * half, half)], preferred_element_type=f32)
+
+        @pl.when(core == part)
+        def _():
+            mine[...] = product
+
+        @pl.when(core != part)
+        def _():
+            theirs[0] = product
+
+    pair = remote(theirs.at[0], theirs.at[1], pair_send, pair_recv, other)
+    pair.start()
+
+    projected[...] = jnp.zeros_like(projected)
+
+    def project(i):
+        query_weight(i).wait()
+        projected[...] += jnp.dot(tok[i], weights[i], preferred_element_type=f32)
+        out_weight(i).start()
+
+    project(me)
+
+    pair.wait_recv()
+    for head in range(chips):
+        fresh_out[head] = (mine[:, head * E:(head + 1) * E] + theirs[1, :, head * E:(head + 1) * E]).astype(bf16)
+    fresh_copies = []
+    for k in range(1, chips):
+        to = index(shifted(k // 2), lax.rem(y + k, 2), 0) // 2
+        copy = remote(fresh_out.at[to], fresh_in.at[chip], fresh_send.at[k], fresh_recv.at[chip], to * 2 + core)
+        copy.start()
+        fresh_copies.append(copy)
+
+    def fwd(i, kz, second):
+        if not second:
+            on = tok_copy(i, n_z - 1 + kz, y_peer)
+            on.start()
+            sends.append(on)
+        on = tok_copy(i, 2 * n_z - 1 + 2 * kz + second, other)
+        on.start()
+        sends.append(on)
+
+    def tok_wait(i):
+        tok_copy(i, 0, other).wait_recv()
+
+    near = [1, n_z - 1] + list(range(2, n_z - 1))
+    for kz in near:
+        i = index(shifted(kz), y, core)
+        tok_wait(i)
+        fwd(i, kz, 0)
+
+    for load in stage_loads + own_loads:
+        load.wait()
+
+    def kv_to(k):
+        to = index(shifted(k // 2), lax.rem(y + k, 2), 0) // 2
+        return remote(stage.at[to], kv.at[me], kv_send.at[k], kv_recv.at[me], to * 2 + core)
+
+    def kv_on(i, k):
+        return remote(kv.at[i], kv.at[i], kv_pass.at[k], kv_recv.at[i], other)
+
+    def kv_wait(i):
+        kv_on(i, 0).wait_recv()
+
+    for k in range(1, chips):
+        kv_to(k).start()
+    kv_on(me, 0).start()
+
+    for kz in [0] + near:
+        i = index(shifted(kz), 1 - y, core)
+        tok_wait(i)
+        fwd(i, kz, 1)
+
+    @pl.loop(1, n_z)
+    def _(kz):
+        project(index(shifted(kz), y, core))
+
+    @pl.loop(0, n_z)
+    def _(kz):
+        project(index(shifted(kz), 1 - y, core))
+
+    @pl.loop(0, chips)
+    def _(k):
+        i = index(shifted(k // 2), lax.rem(y + k, 2), 1 - core)
+        tok_wait(i)
+        project(i)
+
+    for head in range(group):
+        query[head] = (projected[:, head * E:(head + 1) * E] * E ** (-0.5)).astype(bf16)
+
+    new_rows = fresh_out[chip].astype(f32)
+    for k in range(1, chips):
+        source = index(shifted(k // 2), lax.rem(y + k, 2), 0) // 2
+        remote(fresh_out.at[source], fresh_in.at[source], fresh_send.at[0], fresh_recv.at[source], other).wait_recv()
+        new_rows += fresh_in[source].astype(f32)
+    fresh[core] = new_rows.astype(bf16)
+    share = remote(fresh.at[core], fresh.at[core], share_send, share_recv.at[core], other)
+    share.start()
+
+    high[...] = jnp.full_like(high, NEGATIVE_FILL)
+    total[...] = jnp.zeros_like(total)
+    attended[...] = jnp.zeros_like(attended)
+
+    def attend(head, keys, values, masked):
+        scores = lax.dot_general(query[head], keys, (((1,), (1,)), ((), ())), preferred_element_type=f32)
+        scores = masked(scores)
+        before = high[head]
+        after = jnp.maximum(before, jnp.max(scores, axis=1, keepdims=True))
+        high[head] = after
+        scale = jnp.exp(before - after)
+        exponent = jnp.exp(scores - after[:, :1])
+        total[head] = total[head] * scale + jnp.sum(exponent, axis=1, keepdims=True)
+        attended[head] = attended[head] * scale + jnp.dot(
+            exponent.astype(bf16), values, preferred_element_type=f32)
+
+    def attend_block(i):
+        mask = kv[i, pl.ds(2 * slots, MASK_ROWS), :].astype(f32)
+        row = jnp.concatenate([mask[r:r + 1] for r in range(slots // E)], axis=1)
+
+        @pl.loop(0, group)
+        def _(head):
+            attend(head, kv[i, pl.ds(0, slots), :], kv[i, pl.ds(slots, slots), :], lambda s: s + row)
+
+    attend_block(me)
+    remote(fresh.at[1 - core], fresh.at[1 - core], share_send, share_recv.at[1 - core], other).wait_recv()
+
+    @pl.loop(0, group)
+    def _(head):
+        earlier = lax.broadcasted_iota(jnp.int32, (rows, rows), 1) <= lax.broadcasted_iota(jnp.int32, (rows, rows), 0)
+        attend(head, fresh[0], fresh[1], lambda s: jnp.where(earlier, s, NEGATIVE_FILL))
+
+    def source_chip(k):
+        return index(shifted(k // 2), lax.rem(y + k, 2), 0)
+
+    @pl.loop(1, chips)
+    def _(k):
+        i = source_chip(k) + core
+        kv_wait(i)
+        kv_on(i, k).start()
+        attend_block(i)
+        last = source_chip(k - 1) + 1 - core
+        kv_wait(last)
+        attend_block(last)
+
+    last = source_chip(chips - 1) + 1 - core
+    kv_wait(last)
+    attend_block(last)
+
+    for head in range(group):
+        attention[:, head * E:(head + 1) * E] = (attended[head] / total[head]).astype(bf16)
+
+    def product(i):
+        out_weight(i).wait()
+        return jnp.dot(attention[...], weights[i], preferred_element_type=f32)
+
+    def one(slot):
+        return remote(first_out.at[slot], first_in.at[slot], one_send.at[slot], one_recv.at[slot], other)
+
+    def two(zz):
+        return remote(second_out.at[zz], second_in.at[zz], two_send.at[zz], two_recv.at[zz], y_peer)
+
+    def three(zz):
+        return remote(third_out.at[zz], third_in.at[z], three_send.at[zz], three_recv.at[z], index(zz, y, core))
+
+    def first_step(yy):
+        @pl.loop(1, n_z + 1)
+        def _(kz):
+            zz = shifted(kz)
+            slot = zz * 2 + yy
+            first_out[slot] = product(index(zz, yy, 1 - core)).astype(bf16)
+            one(slot).start()
+
+    first_step(1 - y)
+
+    @pl.loop(1, n_z + 1)
+    def _(kz):
+        zz = shifted(kz)
+        slot = zz * 2 + 1 - y
+        value = product(index(zz, 1 - y, core))
+        one(slot).wait_recv()
+        second_out[zz] = (value + first_in[slot].astype(f32)).astype(bf16)
+        two(zz).start()
+
+    first_step(y)
+
+    def summed(zz):
+        slot = zz * 2 + y
+        value = product(index(zz, y, core))
+        one(slot).wait_recv()
+        value += first_in[slot].astype(f32)
+        two(zz).wait_recv()
+        return value + second_in[zz].astype(f32)
+
+    @pl.loop(1, n_z)
+    def _(kz):
+        zz = shifted(kz)
+        third_out[zz] = summed(zz).astype(bf16)
+        three(zz).start()
+
+    projected[...] = summed(z)
+    for kz in range(1, n_z):
+        zz = shifted(kz)
+        remote(third_out.at[zz], third_in.at[zz], three_send.at[zz], three_recv.at[zz], other).wait_recv()
+        projected[...] += third_in[zz].astype(f32)
+    out[...] = projected[...].astype(bf16)
+
+    for copy in sends:
+        copy.wait_send()
+    pair.wait_send()
+    share.wait_send()
+    for copy in fresh_copies:
+        copy.wait_send()
+    for k in range(1, chips):
+        kv_to(k).wait_send()
+    for k in range(chips):
+        kv_on(me, k).wait_send()
+    for slot in range(chips):
+        one(slot).wait_send()
+    for zz in range(n_z):
+        two(zz).wait_send()
+    for kz in range(1, n_z):
+        three(shifted(kz)).wait_send()
+
+
+def fused(tokens, w_query, w_key_value, w_out, cache_keys, cache_values, lengths, offset):
+    devices = lax.axis_size("seq")
+    rows, width = tokens.shape
+    slots, kv_columns = cache_keys.shape
+    n_z = devices // 4
+    chips = devices // 2
+    group = width // E
+    f32, bf16 = jnp.float32, jnp.bfloat16
+    any_space = pl.BlockSpec(memory_space=pl.ANY)
+    smem = pl.BlockSpec(memory_space=pltpu.SMEM)
+    vmem = pltpu.VMEM
+    dma = pltpu.SemaphoreType.DMA
+    block = 2 * slots + MASK_ROWS
+    scratch = [
+        vmem((devices, rows, width), bf16),
+        vmem((devices, width, width), bf16),
+        vmem(w_key_value.shape, bf16),
+        vmem((chips, block, E), bf16),
+        vmem((devices, block, E), bf16),
+        vmem((rows, kv_columns), f32),
+        vmem((2, rows, kv_columns), f32),
+        vmem((chips, rows, E), bf16),
+        vmem((chips, rows, E), bf16),
+        vmem((2, rows, E), bf16),
+        vmem((rows, width), f32),
+        vmem((group, rows, E), bf16),
+        vmem((group, rows, E), f32),
+        vmem((group, rows, E), f32),
+        vmem((group, rows, E), f32),
+        vmem((rows, width), bf16),
+        vmem((chips, rows, width), bf16),
+        vmem((chips, rows, width), bf16),
+        vmem((n_z, rows, width), bf16),
+        vmem((n_z, rows, width), bf16),
+        vmem((n_z, rows, width), bf16),
+        vmem((n_z, rows, width), bf16),
+        dma((4 + 2 * chips,)),
+        dma((devices,)),
+        dma((4 * n_z,)),
+        dma((devices,)),
+        dma((chips,)),
+        dma((devices,)),
+        dma((chips,)),
+        dma,
+        dma,
+        dma((chips,)),
+        dma((chips,)),
+        dma,
+        dma((2,)),
+        dma((chips,)),
+        dma((chips,)),
+        dma((n_z,)),
+        dma((n_z,)),
+        dma((n_z,)),
+        dma((n_z,)),
+    ]
+    return pl.pallas_call(
+        kernel,
+        out_shape=jax.ShapeDtypeStruct((rows, width), bf16),
+        in_specs=[any_space] * 6 + [smem] * 2,
+        out_specs=pl.BlockSpec(memory_space=pltpu.VMEM),
+        scratch_shapes=scratch,
+        compiler_params=pltpu.CompilerParams(
+            collective_id=0, has_side_effects=True, vmem_limit_bytes=58 * 1024 * 1024),
+        cost_estimate=pl.CostEstimate(flops=10 ** 10, bytes_accessed=45 * 10 ** 6, transcendentals=6 * 10 ** 6),
+    )(tokens, w_query, w_key_value, w_out, cache_keys, cache_values, lengths, offset)
 
 
 def local(tokens, w_query, w_key_value, w_out, cache_keys, cache_values, lengths, offset):
@@ -80,4 +466,12 @@
         P("rep"),
     )
     out_specs = P("rep", "seq")
-    return jax.shard_map(local, mesh=mesh, in_specs=in_specs, out_specs=out_specs, check_vma=False)
+    devices = mesh.shape["seq"]
+
+    def body(tokens, w_query, w_key_value, w_out, cache_keys, cache_values, lengths, offset):
+        kv_heads = cache_keys.shape[1] // E
+        chip_per_head = devices == 2 * kv_heads and devices % 4 == 0 and w_query.shape[1] % E == 0
+        form = fused if chip_per_head else local
+        return form(tokens, w_query, w_key_value, w_out, cache_keys, cache_values, lengths, offset)
+
+    return jax.shard_map(body, mesh=mesh, in_specs=in_specs, out_specs=out_specs, check_vma=False)

time: 435 us -> 137 us (0.31)
  blocking collectives: 195 us -> 0 us
  waiting for transfers between devices: 145 us -> 0 us
  Pallas kernels: 0 us -> 134 us
  matrix products: 53.7 us -> 0 us
  other arithmetic: 19.2 us -> 0 us
  between operations: 14.5 us -> 1.3 us
  local copies, waits for them, and re-layouts: 7.69 us -> 1.62 us
    psum x2 -> x0, blocking collectives: 137 us -> none  [the longest x1 77.5 us: local(): lax.psum(jnp.dot(tokens, w_key_value, preferred_element_type=jnp.float32)...]
    pallas_call x0 -> x1, Pallas kernels: none -> 134 us  [fused(): pl.pallas_call(kernel, out_shape=jax.ShapeDtypeStruct((rows, width), bf16...]
    reduce_scatter x2 -> x0, waiting for transfers between devices: 93.2 us -> none  [the longest x1 84.5 us: local(): lax.psum_scatter(jnp.dot(attention, w_out, preferred_element_type=jnp.flo...]
    pmax x1 -> x0, blocking collectives: 57.7 us -> none  [local(): highest = lax.pmax(local_highest, 'seq')]
    dot_general x5 -> x0, matrix products: 53.7 us -> none  [the longest x1 15.8 us: local(): jnp.einsum('hgqp,phe->qhge', weights, value_heads, preferred_element_type...]
    all_gather x2 -> x0, waiting for transfers between devices: 50.6 us -> none  [the longest x1 50.6 us: local(): lax.all_gather(tokens, 'seq', axis=1, tiled=True)]
    reduce_sum x1 -> x0, other arithmetic: 14.8 us -> none  [local(): local_totals = jnp.sum(exponent, axis=-1)]
  transfers between devices with their start and end apart: 4 -> 0, of which waited for: 3 -> 0; matrix products, arithmetic and copies ran while one was open for 5% -> 0% of each run, Pallas kernels for 0% -> 0%
where the time goes in v1:
time: 137 us; the launch traced here: 136 us
  Pallas kernels  134 us (98%)
  local copies, waits for them, and re-layouts  1.62 us (1%)
    pallas_call x1, Pallas kernels, fused(): pl.pallas_call(kernel, out_shape=jax.ShapeDtypeStruct((rows, width), bf16...  134 us

profile of v1, /device:TPU:0, one launch (start us, length us, event | category | flops | bytes accessed | tf_op | source)
XLA Modules:
  0.0 136.4 jit_solution(10572762323999010865)
XLA Ops:
  1.3 133.5 %shard_map.82 = bf16[128,768]{1,0:T(8,128)(2,1)} custom-call(bf16[128,768]{1,0:T(8,128)(2,1)} %tokens.1, bf16[12288,768]{1,0:T(8,128)(2,1)} %w_query.1, bf16[768,2048]{1,0:T(8,128)(2,1)} %w_key_value.1, bf16[768,12288]{1,0:T(8,128)(2,1)} %w_out.1, bf16[512,1024]{1,0:T(8,128)(2,1)} %cache_keys.1, bf16[512,1024]{1,0:T(8,128)(2,1)} %cache_values.1, ...), custom_call_target="tpu_custom_call" | custom-call | flops 10000000000 | bytes 45000000 | tf_op jit(solution)/shard_map/pallas_call | solution.py:386
  134.8 1.6 %copy.12 = bf16[128,768]{1,0:T(8,128)(2,1)} copy(bf16[128,768]{1,0:T(8,128)(2,1)} %shard_map.82) | data formatting | bytes 393216

commit v2 on v1

--- a/solution.py
+++ b/solution.py
@@ -6,7 +6,7 @@
 from jax.sharding import PartitionSpec as P
 
 E = 128
-MASK_ROWS = 16
+COUNT_ROWS = 16
 
 
 NEGATIVE_FILL = -1e30
@@ -95,12 +95,14 @@
     for copy in sends:
         copy.start()
 
-    lane = lax.broadcasted_iota(jnp.int32, (MASK_ROWS, E), 0) * E + lax.broadcasted_iota(jnp.int32, (MASK_ROWS, E), 1)
-    seen = (lane < lengths[0]) & (me * slots + lane < offset[0])
-    bias = jnp.where(seen, 0.0, NEGATIVE_FILL).astype(bf16)
+    filled = jnp.minimum(lengths[0], offset[0] - me * slots)
+    filled = jnp.minimum(jnp.maximum(filled, 0), slots)
+    low = lax.rem(filled, 16)
+    upper = lax.broadcasted_iota(jnp.int32, (COUNT_ROWS, E), 0) < COUNT_ROWS // 2
+    count = jnp.where(upper, filled - low, low).astype(f32).astype(bf16)
     for head in range(chips):
-        stage[head, pl.ds(2 * slots, MASK_ROWS), :] = bias
-    kv[me, pl.ds(2 * slots, MASK_ROWS), :] = bias
+        stage[head, pl.ds(2 * slots, COUNT_ROWS), :] = count
+    kv[me, pl.ds(2 * slots, COUNT_ROWS), :] = count
 
     load_kv.wait()
     for part in range(2):
@@ -191,7 +193,7 @@
         project(i)
 
     for head in range(group):
-        query[head] = (projected[:, head * E:(head + 1) * E] * E ** (-0.5)).astype(bf16)
+        query[head * rows:(head + 1) * rows, :] = (projected[:, head * E:(head + 1) * E] * E ** (-0.5)).astype(bf16)
 
     new_rows = fresh_out[chip].astype(f32)
     for k in range(1, chips):
@@ -205,34 +207,36 @@
     high[...] = jnp.full_like(high, NEGATIVE_FILL)
     total[...] = jnp.zeros_like(total)
     attended[...] = jnp.zeros_like(attended)
-
-    def attend(head, keys, values, masked):
-        scores = lax.dot_general(query[head], keys, (((1,), (1,)), ((), ())), preferred_element_type=f32)
-        scores = masked(scores)
-        before = high[head]
-        after = jnp.maximum(before, jnp.max(scores, axis=1, keepdims=True))
-        high[head] = after
-        scale = jnp.exp(before - after)
-        exponent = jnp.exp(scores - after[:, :1])
-        total[head] = total[head] * scale + jnp.sum(exponent, axis=1, keepdims=True)
-        attended[head] = attended[head] * scale + jnp.dot(
-            exponent.astype(bf16), values, preferred_element_type=f32)
+    pack = 2 if group % 2 == 0 else 1
+    span = pack * rows
+
+    def attend(keys, values, seen):
+        turned = values.T
+        for part in range(group // pack):
+            at = slice(part * span, (part + 1) * span)
+            scores = lax.dot_general(keys, query[at, :], (((1,), (1,)), ((), ())), preferred_element_type=f32)
+            scores = jnp.where(seen, scores, NEGATIVE_FILL)
+            before = high[:, at]
+            after = jnp.maximum(before, jnp.max(scores, axis=0, keepdims=True))
+            high[:, at] = after
+            scale = jnp.exp(before - after)
+            exponent = jnp.exp(scores - after)
+            total[:, at] = total[:, at] * scale + jnp.sum(exponent, axis=0, keepdims=True)
+            attended[:, at] = attended[:, at] * scale + jnp.dot(
+                turned, exponent.astype(bf16), preferred_element_type=f32)
 
     def attend_block(i):
-        mask = kv[i, pl.ds(2 * slots, MASK_ROWS), :].astype(f32)
-        row = jnp.concatenate([mask[r:r + 1] for r in range(slots // E)], axis=1)
-
-        @pl.loop(0, group)
-        def _(head):
-            attend(head, kv[i, pl.ds(0, slots), :], kv[i, pl.ds(slots, slots), :], lambda s: s + row)
+        held = kv[i, pl.ds(2 * slots, COUNT_ROWS), :].astype(f32)
+        filled = (held[:1] + held[COUNT_ROWS // 2:COUNT_ROWS // 2 + 1]).astype(jnp.int32)
+        filled = jnp.concatenate([filled] * pack, axis=1)
+        slot = lax.broadcasted_iota(jnp.int32, (slots, span), 0)
+        attend(kv[i, pl.ds(0, slots), :], kv[i, pl.ds(slots, slots), :], slot < filled)
 
     attend_block(me)
     remote(fresh.at[1 - core], fresh.at[1 - core], share_send, share_recv.at[1 - core], other).wait_recv()
 
-    @pl.loop(0, group)
-    def _(head):
-        earlier = lax.broadcasted_iota(jnp.int32, (rows, rows), 1) <= lax.broadcasted_iota(jnp.int32, (rows, rows), 0)
-        attend(head, fresh[0], fresh[1], lambda s: jnp.where(earlier, s, NEGATIVE_FILL))
+    earlier = lax.broadcasted_iota(jnp.int32, (rows, rows), 0) <= lax.broadcasted_iota(jnp.int32, (rows, rows), 1)
+    attend(fresh[0], fresh[1], jnp.concatenate([earlier] * pack, axis=1))
 
     def source_chip(k):
         return index(shifted(k // 2), lax.rem(y + k, 2), 0)
@@ -252,7 +256,8 @@
     attend_block(last)
 
     for head in range(group):
-        attention[:, head * E:(head + 1) * E] = (attended[head] / total[head]).astype(bf16)
+        at = slice(head * rows, (head + 1) * rows)
+        attention[:, head * E:(head + 1) * E] = (attended[:, at] / total[:, at]).T.astype(bf16)
 
     def product(i):
         out_weight(i).wait()
@@ -339,7 +344,7 @@
     smem = pl.BlockSpec(memory_space=pltpu.SMEM)
     vmem = pltpu.VMEM
     dma = pltpu.SemaphoreType.DMA
-    block = 2 * slots + MASK_ROWS
+    block = 2 * slots + COUNT_ROWS
     scratch = [
         vmem((devices, rows, width), bf16),
         vmem((devices, width, width), bf16),
@@ -352,10 +357,10 @@
         vmem((chips, rows, E), bf16),
         vmem((2, rows, E), bf16),
         vmem((rows, width), f32),
-        vmem((group, rows, E), bf16),
-        vmem((group, rows, E), f32),
-        vmem((group, rows, E), f32),
-        vmem((group, rows, E), f32),
+        vmem((group * rows, E), bf16),
+        vmem((1, group * rows), f32),
+        vmem((1, group * rows), f32),
+        vmem((E, group * rows), f32),
         vmem((rows, width), bf16),
         vmem((chips, rows, width), bf16),
         vmem((chips, rows, width), bf16),

time: 137 us -> 118 us (0.86)
  Pallas kernels: 134 us -> 115 us
    pallas_call x1, Pallas kernels: 134 us -> 115 us  [fused(): pl.pallas_call(kernel, out_shape=jax.ShapeDtypeStruct((rows, width), bf16...]
where the time goes in v2:
time: 118 us
  Pallas kernels  115 us (97%)
  local copies, waits for them, and re-layouts  1.62 us (1%)
  between operations  1.3 us (1%)
    pallas_call x1, Pallas kernels, fused(): pl.pallas_call(kernel, out_shape=jax.ShapeDtypeStruct((rows, width), bf16...  115 us

profile of v2, /device:TPU:0, one launch (start us, length us, event | category | flops | bytes accessed | tf_op | source)
XLA Modules:
  0.0 118.3 jit_solution(14636122339735316008)
XLA Ops:
  1.3 115.4 %shard_map.82 = bf16[128,768]{1,0:T(8,128)(2,1)} custom-call(bf16[128,768]{1,0:T(8,128)(2,1)} %tokens.1, bf16[12288,768]{1,0:T(8,128)(2,1)} %w_query.1, bf16[768,2048]{1,0:T(8,128)(2,1)} %w_key_value.1, bf16[768,12288]{1,0:T(8,128)(2,1)} %w_out.1, bf16[512,1024]{1,0:T(8,128)(2,1)} %cache_keys.1, bf16[512,1024]{1,0:T(8,128)(2,1)} %cache_values.1, ...), custom_call_target="tpu_custom_call" | custom-call | flops 10000000000 | bytes 45000000 | tf_op jit(solution)/shard_map/pallas_call | solution.py:391
  116.7 1.6 %copy.12 = bf16[128,768]{1,0:T(8,128)(2,1)} copy(bf16[128,768]{1,0:T(8,128)(2,1)} %shard_map.82) | data formatting | bytes 393216
